TPU v7x, 32 devices: a whole 2x2x4 slice. The times are simulated.
32 devices in a mesh: scen: 2 (over y), tm: 8 (over z, x), xfmr: 2 (over core).
Axes of the slice: x: 2, y: 2, z: 4, core: 2. Of those that a mesh axis runs over, the one named last changes fastest.
Arguments:
- voltages: bfloat16 [8, 512, 8192], P('scen', 'tm', 'xfmr'), parts along dimension 0, may hold values from -6 to 6
- coupling: bfloat16 [96, 4, 128, 128], P('xfmr'), may hold values from -0.25 to 0.25
- pattern: int32 [96, 4], P('xfmr'), may hold values from 0 to 63
- substation: int32 [12288], P('xfmr'), may hold values from 0 to 255
- time_const: float32 [256, 2], replicated, may hold values from 30 to 2048
- amplitude: float32 [256, 2], replicated, may hold values from 0.5 to 2
Outputs:
- hot_spot: bfloat16 [8, 512, 12288], P('scen', 'tm', 'xfmr'), parts along dimension 0
There are 2 independent parts, one for each index of `scen`. A program takes and returns all parts, laid end to end along the dimension named above; an argument that names none is the same for every part. Nothing has to cross between parts.
All inputs are finite; a program needn't handle non-finite values.
Results may differ from a plain program's by a relative error of at most 0.002.
Values may be sent and summed in bfloat16 or wider, within the bound.
A program may use at most 128 MiB of HBM per device.

v0:
```python
import functools
import jax
import jax.numpy as jnp
from jax import lax
from jax.experimental import pallas as pl
from jax.experimental.pallas import tpu as pltpu
from jax.sharding import PartitionSpec as P

MESH = pl.DeviceIdType.MESH
CHUNK = 8


def kernel(
    pairs, volt_ref, coup_ref, pat_ref, sub_ref, tc_ref, amp_ref, out_ref,
    vbuf, cbuf, hbuf, grow, fade, ends, peer_ends, chain_in, chain_out, carry, span, once,
    tab, lower, obuf,
    volt_sem, coup_sem, out_sem, gather_send, gather_recv, peer_send, peer_recv, chain_send, chain_recv,
):
    scen, steps, lines = volt_ref.shape
    blocks, depth, width = coup_ref.shape
    rows = scen * steps
    groups = tc_ref.shape[1]
    slots = pat_ref.shape[1]
    panel = depth // slots
    chunks = blocks // CHUNK
    core = lax.axis_index("xfmr")
    me = lax.axis_index("tm")
    pair = me // 2
    odd = me % 2
    partner = me + 1 - 2 * odd
    has_prev = pair > 0
    has_next = pair < pairs - 1

    barrier = pltpu.get_barrier_semaphore()
    pl.semaphore_signal(barrier, inc=1, device_id={"xfmr": 1 - core}, device_id_type=MESH)
    pl.semaphore_signal(barrier, inc=1, device_id={"tm": partner}, device_id_type=MESH)

    @pl.when(has_prev)
    def _():
        pl.semaphore_signal(barrier, inc=1, device_id={"tm": me - 2}, device_id_type=MESH)

    @pl.when(has_next)
    def _():
        pl.semaphore_signal(barrier, inc=1, device_id={"tm": me + 2}, device_id_type=MESH)

    panels = lines // panel

    def local_panel(n):
        return pltpu.make_async_copy(
            volt_ref.at[:, :, pl.ds(pl.multiple_of(n * panel, panel), panel)],
            vbuf.at[core * panels + n],
            volt_sem.at[n],
        )

    def sent_panel(n):
        return pltpu.make_async_remote_copy(
            src_ref=volt_ref.at[:, :, pl.ds(pl.multiple_of(n * panel, panel), panel)],
            dst_ref=vbuf.at[core * panels + n],
            send_sem=gather_send.at[n],
            recv_sem=gather_recv.at[n],
            device_id={"xfmr": 1 - core},
            device_id_type=MESH,
        )

    def start_local(n, _):
        local_panel(n).start()
        return 0

    def start_sent(n, _):
        sent_panel(n).start()
        return 0

    def wait_panels(n, _):
        local_panel(n).wait()
        sent_panel(n).wait()
        return 0

    local_coup = pltpu.make_async_copy(coup_ref, cbuf, coup_sem)
    pl.semaphore_wait(barrier, 2 + has_prev.astype(jnp.int32) + has_next.astype(jnp.int32))
    lax.fori_loop(0, panels, start_sent, 0)
    lax.fori_loop(0, panels, start_local, 0)
    local_coup.start()

    tab[...] = jnp.zeros_like(tab)
    tab[0:2, :] = 1.0 / tc_ref[...]
    tab[2:4, :] = amp_ref[...]
    whole = tab[0:4, :]
    high = whole.astype(jnp.bfloat16).astype(jnp.float32)
    middle = (whole - high).astype(jnp.bfloat16).astype(jnp.float32)
    tab[0:4, :] = high
    tab[4:8, :] = middle
    tab[8:12, :] = whole - high - middle
    i = lax.broadcasted_iota(jnp.int32, (rows, rows), 0)
    j = lax.broadcasted_iota(jnp.int32, (rows, rows), 1)
    keep = jnp.where((i // steps == j // steps) & (j <= i), 1.0, 0.0).astype(jnp.bfloat16)
    lower[:, 0:rows] = keep
    lower[:, rows:] = keep

    def prepare(b, _):
        k, lanes = b // CHUNK, pl.ds(pl.multiple_of((b % CHUNK) * width, width), width)
        station = sub_ref[pl.ds(b, 1), :]
        onehot = jnp.where(
            lax.broadcasted_iota(jnp.int32, (groups, width), 0) == station, 1.0, 0.0
        ).astype(jnp.bfloat16)
        parts = jnp.dot(tab[...].astype(jnp.bfloat16), onehot, preferred_element_type=jnp.float32)
        found = parts[0:4] + parts[4:8] + parts[8:12]
        t = lax.broadcasted_iota(jnp.int32, (steps, width), 0).astype(jnp.float32)
        for r in range(2):
            rate = found[r : r + 1]
            decay = jnp.exp(-rate)
            scale = found[2 + r : 3 + r] * (1.0 - decay)
            grow[b, r] = jnp.exp(t * rate)
            fade[b, r] = jnp.exp(-t * rate) * scale
            span[k, scen * r : scen * (r + 1), lanes] = jnp.broadcast_to(
                jnp.exp(-float(steps) * rate), (scen, width)
            )
            once[k, scen * r : scen * (r + 1), lanes] = jnp.broadcast_to(decay, (scen, width))
        return 0

    lax.fori_loop(0, blocks, prepare, 0, unroll=2)

    local_coup.wait()
    lax.fori_loop(0, panels, wait_panels, 0)

    def peer_copy(k):
        return pltpu.make_async_remote_copy(
            src_ref=ends.at[k], dst_ref=peer_ends.at[k],
            send_sem=peer_send.at[k], recv_sem=peer_recv.at[k],
            device_id={"tm": partner}, device_id_type=MESH,
        )

    def chain_copy(k):
        return pltpu.make_async_remote_copy(
            src_ref=chain_out.at[k], dst_ref=chain_in.at[k],
            send_sem=chain_send.at[k], recv_sem=chain_recv.at[k],
            device_id={"tm": me + 2}, device_id_type=MESH,
        )

    def couple(k, _):
        def one(n, _):
            b = k * CHUNK + n
            lanes = pl.ds(pl.multiple_of(n * width, width), width)
            picked = jnp.concatenate(
                [
                    vbuf[pat_ref[b, slot]].reshape(rows, panel)
                    for slot in range(slots)
                ],
                axis=1,
            )
            current = jnp.dot(picked, cbuf[b], preferred_element_type=jnp.float32)
            heat = jnp.abs(current).astype(jnp.bfloat16)
            hbuf[b] = heat
            heat = heat.astype(jnp.float32).reshape(scen, steps, width)
            for r in range(2):
                top = grow[b, r]
                total = jnp.sum(heat * top[None], axis=1)
                ends[k, scen * r : scen * (r + 1), lanes] = total / top[steps - 1 : steps]
            return 0

        lax.fori_loop(0, CHUNK, one, 0, unroll=2)
        peer_copy(k).start()
        return 0

    lax.fori_loop(0, chunks, couple, 0)

    @pl.when(jnp.logical_not(has_prev))
    def _():
        chain_in[...] = jnp.zeros_like(chain_in)

    def finish(k, _):
        peer_copy(k).wait_recv()

        @pl.when(has_prev)
        def _():
            chain_copy(k).wait_recv()

        first = jnp.where(odd == 0, ends[k], peer_ends[k])
        second = jnp.where(odd == 0, peer_ends[k], ends[k])
        over = span[k]
        came = chain_in[k]
        middle = over * came + first

        @pl.when(has_next)
        def _():
            chain_out[k] = over * middle + second
            chain_copy(k).start()

        carry[...] = once[k] * jnp.where(odd == 0, came, middle)

        def one(n, _):
            b = k * CHUNK + n
            lanes = pl.ds(pl.multiple_of(n * width, width), width)
            heat = hbuf[b].astype(jnp.float32).reshape(scen, steps, width)
            highs, lows = [], []
            for r in range(2):
                grown = (heat * grow[b, r][None]).reshape(rows, width)
                high = grown.astype(jnp.bfloat16)
                highs.append(high)
                lows.append((grown - high.astype(jnp.float32)).astype(jnp.bfloat16))
            right = jnp.concatenate(
                [jnp.concatenate(highs, axis=1), jnp.concatenate(lows, axis=1)], axis=0
            )
            summed = jnp.dot(lower[...], right, preferred_element_type=jnp.float32)
            total = None
            for r in range(2):
                part = summed[:, r * width : (r + 1) * width].reshape(scen, steps, width)
                begun = carry[scen * r : scen * (r + 1), lanes]
                term = fade[b, r][None] * (part + begun[:, None, :])
                total = term if total is None else total + term
            obuf[k, :, :, lanes] = total.astype(jnp.bfloat16)
            return 0

        lax.fori_loop(0, CHUNK, one, 0, unroll=2)
        out_copy(k).start()
        return 0

    def out_copy(k):
        span_lanes = CHUNK * width
        return pltpu.make_async_copy(
            obuf.at[k],
            out_ref.at[:, :, pl.ds(pl.multiple_of(k * span_lanes, span_lanes), span_lanes)],
            out_sem.at[k],
        )

    lax.fori_loop(0, chunks, finish, 0)

    def drain(k, _):
        out_copy(k).wait()
        peer_copy(k).wait_send()

        @pl.when(has_next)
        def _():
            chain_copy(k).wait_send()

        return 0

    lax.fori_loop(0, chunks, drain, 0)


def body(pairs, voltages, coupling, pattern, substation, time_const, amplitude):
    scen, steps, lines = voltages.shape
    blocks, slots, panel, width = coupling.shape
    chunks = blocks // CHUNK
    lanes = CHUNK * width
    rows = scen * steps
    state = (chunks, 2 * scen, lanes)
    vmem = pl.BlockSpec(memory_space=pltpu.VMEM)
    hbm = pl.BlockSpec(memory_space=pl.ANY)
    dma = pltpu.SemaphoreType.DMA
    return pl.pallas_call(
        functools.partial(kernel, pairs),
        out_shape=jax.ShapeDtypeStruct((scen, steps, blocks * width), jnp.bfloat16),
        in_specs=[hbm, hbm, pl.BlockSpec(memory_space=pltpu.SMEM), vmem, vmem, vmem],
        out_specs=hbm,
        scratch_shapes=[
            pltpu.VMEM((2 * lines // panel, scen, steps, panel), jnp.bfloat16),
            pltpu.VMEM((blocks, slots * panel, width), jnp.bfloat16),
            pltpu.VMEM((blocks, rows, width), jnp.bfloat16),
            pltpu.VMEM((blocks, 2, steps, width), jnp.float32),
            pltpu.VMEM((blocks, 2, steps, width), jnp.float32),
            pltpu.VMEM(state, jnp.float32),
            pltpu.VMEM(state, jnp.float32),
            pltpu.VMEM(state, jnp.float32),
            pltpu.VMEM(state, jnp.float32),
            pltpu.VMEM(state[1:], jnp.float32),
            pltpu.VMEM(state, jnp.float32),
            pltpu.VMEM(state, jnp.float32),
            pltpu.VMEM((16, time_const.shape[0]), jnp.float32),
            pltpu.VMEM((rows, 2 * rows), jnp.bfloat16),
            pltpu.VMEM((chunks, scen, steps, lanes), jnp.bfloat16),
            dma((lines // panel,)),
            dma,
            dma((chunks,)),
            dma((lines // panel,)),
            dma((lines // panel,)),
            dma((chunks,)),
            dma((chunks,)),
            dma((chunks,)),
            dma((chunks,)),
        ],
        compiler_params=pltpu.CompilerParams(
            collective_id=0, has_side_effects=True, vmem_limit_bytes=48 * 1024 * 1024
        ),
    )(
        voltages,
        coupling.reshape(blocks, slots * panel, width),
        pattern,
        substation.reshape(blocks, width),
        time_const.T,
        amplitude.T,
    )


def solution(mesh):
    in_specs = (
        P("scen", "tm", "xfmr"),
        P("xfmr", None, None, None),
        P("xfmr", None),
        P("xfmr"),
        P(),
        P(),
    )
    out_specs = P("scen", "tm", "xfmr")
    return jax.shard_map(
        functools.partial(body, mesh.shape["tm"] // 2),
        mesh=mesh, in_specs=in_specs, out_specs=out_specs, check_vma=False,
    )
```

profile of v0, /device:TPU:26, one launch (start us, length us, event | category | flops | bytes accessed | tf_op | source)
XLA Modules:
  0.0 38.6 jit_solution(5518435584045496657)
XLA Ops:
  0.0 0.8 %copy.7.pat_ref = s32[48,4]{1,0:T(8,128)S(1)} copy(s32[48,4]{0,1:T(4,128)} %param.8) | data formatting | bytes 1536 | tf_op args[2]
  0.8 0.0 copy-start
  0.8 1.6 %copy-done = bf16[4,64,4096]{2,1,0:T(8,128)(2,1)S(1)} copy-done((bf16[4,64,4096]{2,1,0:T(8,128)(2,1)S(1)}, bf16[4,64,4096]{2,1,0:T(8,128)(2,1)}, u32[]{:S(2)}) %copy-start) | copy-done | bytes 2097176
  2.4 0.0 copy-start.1
  2.4 0.7 %copy-done.1 = s32[6144]{0:T(1024)S(1)} copy-done((s32[6144]{0:T(1024)S(1)}, s32[6144]{0:T(1024)}, u32[]{:S(2)}) %copy-start.1) | copy-done | bytes 24600
  3.1 0.0 copy-start.2
  3.1 0.7 %copy-done.2 = f32[256,2]{0,1:T(2,128)S(1)} copy-done((f32[256,2]{0,1:T(2,128)S(1)}, f32[256,2]{0,1:T(2,128)}, u32[]{:S(2)}) %copy-start.2) | copy-done | bytes 2072
  3.8 0.0 copy-start.3
  3.8 0.7 %copy-done.3 = f32[256,2]{0,1:T(2,128)S(1)} copy-done((f32[256,2]{0,1:T(2,128)S(1)}, f32[256,2]{0,1:T(2,128)}, u32[]{:S(2)}) %copy-start.3) | copy-done | bytes 2072
  4.5 32.5 %shard_map.64 = bf16[4,64,6144]{2,1,0:T(8,128)(2,1)S(1)} custom-call(bf16[4,64,4096]{2,1,0:T(8,128)(2,1)S(1)} %copy-done, bf16[48,512,128]{2,1,0:T(8,128)(2,1)} %bitcast.7, s32[48,4]{1,0:T(8,128)S(1)} %copy.7.pat_ref, s32[48,128]{1,0:T(8,128)S(1)} %bitcast.4, f32[2,256]{1,0:T(2,128)S(1)} %bitcast.5, f32[2,256]{1,0:T(2,128)S(1)} %bitcast.6), custom_call_target="tpu_custom_call" | custom-call | tf_op jit(solution)/shard_map/pallas_call | solution.py:250
  36.9 1.7 %copy.9 = bf16[4,64,6144]{2,1,0:T(8,128)(2,1)} copy(bf16[4,64,6144]{2,1,0:T(8,128)(2,1)S(1)} %shard_map.64) | data formatting | bytes 6291456
Async XLA Ops:
  0.8 1.6 %copy-start = (bf16[4,64,4096]{2,1,0:T(8,128)(2,1)S(1)}, bf16[4,64,4096]{2,1,0:T(8,128)(2,1)}, u32[]{:S(2)}) copy-start(bf16[4,64,4096]{2,1,0:T(8,128)(2,1)} %volt_ref.1) | copy-start | bytes 6291460
  2.4 0.7 %copy-start.1 = (s32[6144]{0:T(1024)S(1)}, s32[6144]{0:T(1024)}, u32[]{:S(2)}) copy-start(s32[6144]{0:T(1024)} %param.9) | copy-start | bytes 73732
  3.1 0.7 %copy-start.2 = (f32[256,2]{0,1:T(2,128)S(1)}, f32[256,2]{0,1:T(2,128)}, u32[]{:S(2)}) copy-start(f32[256,2]{0,1:T(2,128)} %param.10) | copy-start | bytes 6148
  3.8 0.7 %copy-start.3 = (f32[256,2]{0,1:T(2,128)S(1)}, f32[256,2]{0,1:T(2,128)}, u32[]{:S(2)}) copy-start(f32[256,2]{0,1:T(2,128)} %param.11) | copy-start | bytes 6148
where the time goes:
time: 38.9 us; the launch traced here: 38.6 us
  Pallas kernels  32.5 us (84%)
  local copies, waits for them, and re-layouts  6.12 us (16%)
    pallas_call x1, Pallas kernels, body(): pl.pallas_call(functools.partial(kernel, pairs), out_shape=jax.ShapeDtype...  32.5 us
    unnamed x10, local copies, waits for them, and re-layouts  6.12 us

commit v1 on v0

--- a/solution.py
+++ b/solution.py
@@ -7,20 +7,26 @@
 from jax.sharding import PartitionSpec as P
 
 MESH = pl.DeviceIdType.MESH
-CHUNK = 8
+CHUNK = 4
+UNROLL_A = 4
+UNROLL_B = 4
+UNROLL_C = 4
+UNROLL_P = 4
+LAG = 8
+LAG_PAIR = 4
 
 
 def kernel(
-    pairs, volt_ref, coup_ref, pat_ref, sub_ref, tc_ref, amp_ref, out_ref,
-    vbuf, cbuf, hbuf, grow, fade, ends, peer_ends, chain_in, chain_out, carry, span, once,
-    tab, lower, obuf,
-    volt_sem, coup_sem, out_sem, gather_send, gather_recv, peer_send, peer_recv, chain_send, chain_recv,
+    pairs, volt_ref, coup_ref, pat_hbm, sub_hbm, tc_hbm, amp_hbm, out_ref,
+    pat_ref, sub_ref, tc_ref, amp_ref, vbuf, cbuf, hbuf, grow, fade, ends, peer_ends, chain_in, chain_out, carry, span, once,
+    tab, lower, lbuf, obuf,
+    small_sem, volt_sem, coup_sem, out_sem, gather_send, gather_recv, peer_send, peer_recv, chain_send, chain_recv,
 ):
     scen, steps, lines = volt_ref.shape
     blocks, depth, width = coup_ref.shape
     rows = scen * steps
     groups = tc_ref.shape[1]
-    slots = pat_ref.shape[1]
+    slots = pat_ref.shape[0]
     panel = depth // slots
     chunks = blocks // CHUNK
     core = lax.axis_index("xfmr")
@@ -75,11 +81,22 @@
         sent_panel(n).wait()
         return 0
 
+    smalls = [
+        pltpu.make_async_copy(source, target, small_sem.at[n])
+        for n, (source, target) in enumerate(
+            ((tc_hbm, tc_ref), (amp_hbm, amp_ref), (sub_hbm, sub_ref), (pat_hbm, pat_ref))
+        )
+    ]
+    for copy in smalls:
+        copy.start()
     local_coup = pltpu.make_async_copy(coup_ref, cbuf, coup_sem)
+    local_coup.start()
+    lax.fori_loop(0, panels, start_local, 0)
     pl.semaphore_wait(barrier, 2 + has_prev.astype(jnp.int32) + has_next.astype(jnp.int32))
     lax.fori_loop(0, panels, start_sent, 0)
-    lax.fori_loop(0, panels, start_local, 0)
-    local_coup.start()
+
+    for copy in smalls:
+        copy.wait()
 
     tab[...] = jnp.zeros_like(tab)
     tab[0:2, :] = 1.0 / tc_ref[...]
@@ -90,11 +107,10 @@
     tab[0:4, :] = high
     tab[4:8, :] = middle
     tab[8:12, :] = whole - high - middle
-    i = lax.broadcasted_iota(jnp.int32, (rows, rows), 0)
-    j = lax.broadcasted_iota(jnp.int32, (rows, rows), 1)
-    keep = jnp.where((i // steps == j // steps) & (j <= i), 1.0, 0.0).astype(jnp.bfloat16)
-    lower[:, 0:rows] = keep
-    lower[:, rows:] = keep
+    i = lax.broadcasted_iota(jnp.int32, lower.shape, 0)
+    j = lax.broadcasted_iota(jnp.int32, lower.shape, 1)
+    keep = (i // steps == j // (2 * steps)) & (j % steps <= i % steps)
+    lower[...] = jnp.where(keep, 1.0, 0.0).astype(jnp.bfloat16)
 
     def prepare(b, _):
         k, lanes = b // CHUNK, pl.ds(pl.multiple_of((b % CHUNK) * width, width), width)
@@ -117,7 +133,7 @@
             once[k, scen * r : scen * (r + 1), lanes] = jnp.broadcast_to(decay, (scen, width))
         return 0
 
-    lax.fori_loop(0, blocks, prepare, 0, unroll=2)
+    lax.fori_loop(0, blocks, prepare, 0, unroll=UNROLL_P)
 
     local_coup.wait()
     lax.fori_loop(0, panels, wait_panels, 0)
@@ -136,13 +152,13 @@
             device_id={"tm": me + 2}, device_id_type=MESH,
         )
 
-    def couple(k, _):
+    def couple(k):
         def one(n, _):
             b = k * CHUNK + n
             lanes = pl.ds(pl.multiple_of(n * width, width), width)
             picked = jnp.concatenate(
                 [
-                    vbuf[pat_ref[b, slot]].reshape(rows, panel)
+                    vbuf[pat_ref[slot, b]].reshape(rows, panel)
                     for slot in range(slots)
                 ],
                 axis=1,
@@ -157,17 +173,14 @@
                 ends[k, scen * r : scen * (r + 1), lanes] = total / top[steps - 1 : steps]
             return 0
 
-        lax.fori_loop(0, CHUNK, one, 0, unroll=2)
+        lax.fori_loop(0, CHUNK, one, 0, unroll=UNROLL_A)
         peer_copy(k).start()
-        return 0
-
-    lax.fori_loop(0, chunks, couple, 0)
 
     @pl.when(jnp.logical_not(has_prev))
     def _():
         chain_in[...] = jnp.zeros_like(chain_in)
 
-    def finish(k, _):
+    def advance(k):
         peer_copy(k).wait_recv()
 
         @pl.when(has_prev)
@@ -185,34 +198,7 @@
             chain_out[k] = over * middle + second
             chain_copy(k).start()
 
-        carry[...] = once[k] * jnp.where(odd == 0, came, middle)
-
-        def one(n, _):
-            b = k * CHUNK + n
-            lanes = pl.ds(pl.multiple_of(n * width, width), width)
-            heat = hbuf[b].astype(jnp.float32).reshape(scen, steps, width)
-            highs, lows = [], []
-            for r in range(2):
-                grown = (heat * grow[b, r][None]).reshape(rows, width)
-                high = grown.astype(jnp.bfloat16)
-                highs.append(high)
-                lows.append((grown - high.astype(jnp.float32)).astype(jnp.bfloat16))
-            right = jnp.concatenate(
-                [jnp.concatenate(highs, axis=1), jnp.concatenate(lows, axis=1)], axis=0
-            )
-            summed = jnp.dot(lower[...], right, preferred_element_type=jnp.float32)
-            total = None
-            for r in range(2):
-                part = summed[:, r * width : (r + 1) * width].reshape(scen, steps, width)
-                begun = carry[scen * r : scen * (r + 1), lanes]
-                term = fade[b, r][None] * (part + begun[:, None, :])
-                total = term if total is None else total + term
-            obuf[k, :, :, lanes] = total.astype(jnp.bfloat16)
-            return 0
-
-        lax.fori_loop(0, CHUNK, one, 0, unroll=2)
-        out_copy(k).start()
-        return 0
+        carry[k] = once[k] * jnp.where(odd == 0, came, middle)
 
     def out_copy(k):
         span_lanes = CHUNK * width
@@ -222,7 +208,76 @@
             out_sem.at[k],
         )
 
-    lax.fori_loop(0, chunks, finish, 0)
+    def convolve(k):
+        def one(n, _):
+            b = k * CHUNK + n
+            lanes = pl.ds(pl.multiple_of(n * width, width), width)
+            for s in range(0, scen, 2):
+                columns = []
+                for r in range(2):
+                    parts = []
+                    for u in (s, s + 1):
+                        heat = hbuf[b, u * steps : (u + 1) * steps].astype(jnp.float32)
+                        grown = heat * grow[b, r]
+                        high = grown.astype(jnp.bfloat16)
+                        parts.append(high)
+                        parts.append((grown - high.astype(jnp.float32)).astype(jnp.bfloat16))
+                    columns.append(jnp.concatenate(parts, axis=0))
+                summed = jnp.dot(
+                    lower[...], jnp.concatenate(columns, axis=1), preferred_element_type=jnp.float32
+                )
+                for v in range(2):
+                    total = None
+                    for r in range(2):
+                        part = summed[v * steps : (v + 1) * steps, r * width : (r + 1) * width]
+                        term = fade[b, r] * part
+                        total = term if total is None else total + term
+                    lbuf[b, s + v] = total
+            return 0
+
+        lax.fori_loop(0, CHUNK, one, 0, unroll=UNROLL_B)
+
+    def combine(k):
+        def one(n, _):
+            b = k * CHUNK + n
+            lanes = pl.ds(pl.multiple_of(n * width, width), width)
+            for s in range(scen):
+                total = lbuf[b, s]
+                for r in range(2):
+                    row = scen * r + s
+                    total = total + fade[b, r] * carry[k, row : row + 1, lanes]
+                obuf[k, s, :, lanes] = total.astype(jnp.bfloat16)
+            return 0
+
+        lax.fori_loop(0, CHUNK, one, 0, unroll=UNROLL_C)
+        out_copy(k).start()
+
+    lag = jnp.minimum(LAG + LAG_PAIR * pair, 2 * chunks)
+    delay = jnp.maximum(lag, chunks)
+
+    def step(n, _):
+        late = n - lag
+        last = n - delay
+
+        @pl.when((late >= 0) & (late < chunks))
+        def _():
+            advance(late)
+
+        @pl.when(n < chunks)
+        def _():
+            couple(n)
+
+        @pl.when((n >= chunks) & (n < 2 * chunks))
+        def _():
+            convolve(n - chunks)
+
+        @pl.when(last >= 0)
+        def _():
+            combine(last)
+
+        return 0
+
+    lax.fori_loop(0, chunks + delay, step, 0)
 
     def drain(k, _):
         out_copy(k).wait()
@@ -244,15 +299,18 @@
     lanes = CHUNK * width
     rows = scen * steps
     state = (chunks, 2 * scen, lanes)
-    vmem = pl.BlockSpec(memory_space=pltpu.VMEM)
-    hbm = pl.BlockSpec(memory_space=pl.ANY)
+    hbm = pl.BlockSpec(memory_space=pltpu.HBM)
     dma = pltpu.SemaphoreType.DMA
     return pl.pallas_call(
         functools.partial(kernel, pairs),
-        out_shape=jax.ShapeDtypeStruct((scen, steps, blocks * width), jnp.bfloat16),
-        in_specs=[hbm, hbm, pl.BlockSpec(memory_space=pltpu.SMEM), vmem, vmem, vmem],
-        out_specs=hbm,
+        out_shape=pltpu.VMEM((scen, steps, blocks * width), jnp.bfloat16),
+        in_specs=[hbm] * 6,
+        out_specs=pl.BlockSpec(memory_space=pl.ANY),
         scratch_shapes=[
+            pltpu.SMEM((slots, blocks), jnp.int32),
+            pltpu.VMEM((blocks, width), jnp.int32),
+            pltpu.VMEM(time_const.shape[::-1], jnp.float32),
+            pltpu.VMEM(amplitude.shape[::-1], jnp.float32),
             pltpu.VMEM((2 * lines // panel, scen, steps, panel), jnp.bfloat16),
             pltpu.VMEM((blocks, slots * panel, width), jnp.bfloat16),
             pltpu.VMEM((blocks, rows, width), jnp.bfloat16),
@@ -262,12 +320,14 @@
             pltpu.VMEM(state, jnp.float32),
             pltpu.VMEM(state, jnp.float32),
             pltpu.VMEM(state, jnp.float32),
-            pltpu.VMEM(state[1:], jnp.float32),
+            pltpu.VMEM(state, jnp.float32),
             pltpu.VMEM(state, jnp.float32),
             pltpu.VMEM(state, jnp.float32),
             pltpu.VMEM((16, time_const.shape[0]), jnp.float32),
-            pltpu.VMEM((rows, 2 * rows), jnp.bfloat16),
+            pltpu.VMEM((2 * steps, 4 * steps), jnp.bfloat16),
+            pltpu.VMEM((blocks, scen, steps, width), jnp.float32),
             pltpu.VMEM((chunks, scen, steps, lanes), jnp.bfloat16),
+            dma((4,)),
             dma((lines // panel,)),
             dma,
             dma((chunks,)),
@@ -279,12 +339,12 @@
             dma((chunks,)),
         ],
         compiler_params=pltpu.CompilerParams(
-            collective_id=0, has_side_effects=True, vmem_limit_bytes=48 * 1024 * 1024
+            collective_id=0, has_side_effects=True, vmem_limit_bytes=60 * 1024 * 1024
         ),
     )(
         voltages,
         coupling.reshape(blocks, slots * panel, width),
-        pattern,
+        pattern.T,
         substation.reshape(blocks, width),
         time_const.T,
         amplitude.T,

time: 38.9 us -> 24.7 us (0.63)
  Pallas kernels: 32.5 us -> 22.7 us
  local copies, waits for them, and re-layouts: 6.12 us -> 1.67 us
    pallas_call x1, Pallas kernels: 32.5 us -> 22.7 us  [body(): pl.pallas_call(functools.partial(kernel, pairs), out_shape=pltpu.VMEM((sc...]
    unnamed x10 -> x1, local copies, waits for them, and re-layouts: 6.12 us -> 1.67 us
where the time goes in v1:
time: 24.7 us; the launch traced here: 24.4 us
  Pallas kernels  22.7 us (92%)
  local copies, waits for them, and re-layouts  1.67 us (7%)
    pallas_call x1, Pallas kernels, body(): pl.pallas_call(functools.partial(kernel, pairs), out_shape=pltpu.VMEM((sc...  22.7 us
    unnamed x1, local copies, waits for them, and re-layouts  1.67 us

profile of v1, /device:TPU:26, one launch (start us, length us, event | category | flops | bytes accessed | tf_op | source)
XLA Modules:
  0.0 24.4 jit_solution(8603514153579742863)
XLA Ops:
  0.0 22.7 %shard_map.64 = bf16[4,64,6144]{2,1,0:T(8,128)(2,1)S(1)} custom-call(bf16[4,64,4096]{2,1,0:T(8,128)(2,1)} %volt_ref.1, bf16[48,512,128]{2,1,0:T(8,128)(2,1)} %bitcast.5, s32[4,48]{1,0:T(4,128)} %bitcast.7, s32[48,128]{1,0:T(8,128)} %bitcast.6, f32[2,256]{1,0:T(2,128)} %bitcast.8, f32[2,256]{1,0:T(2,128)} %bitcast.9), custom_call_target="tpu_custom_call" | custom-call | tf_op jit(solution)/shard_map/pallas_call | solution.py:304
  22.7 1.7 %copy.8 = bf16[4,64,6144]{2,1,0:T(8,128)(2,1)} copy(bf16[4,64,6144]{2,1,0:T(8,128)(2,1)S(1)} %shard_map.64) | data formatting | bytes 6291456

commit v2 on v1

--- a/solution.py
+++ b/solution.py
@@ -19,8 +19,8 @@
 def kernel(
     pairs, volt_ref, coup_ref, pat_hbm, sub_hbm, tc_hbm, amp_hbm, out_ref,
     pat_ref, sub_ref, tc_ref, amp_ref, vbuf, cbuf, hbuf, grow, fade, ends, peer_ends, chain_in, chain_out, carry, span, once,
-    tab, lower, lbuf, obuf,
-    small_sem, volt_sem, coup_sem, out_sem, gather_send, gather_recv, peer_send, peer_recv, chain_send, chain_recv,
+    tab, lower, lbuf,
+    small_sem, volt_sem, coup_sem, gather_send, gather_recv, peer_send, peer_recv, chain_send, chain_recv,
 ):
     scen, steps, lines = volt_ref.shape
     blocks, depth, width = coup_ref.shape
@@ -199,14 +199,6 @@
             chain_copy(k).start()
 
         carry[k] = once[k] * jnp.where(odd == 0, came, middle)
-
-    def out_copy(k):
-        span_lanes = CHUNK * width
-        return pltpu.make_async_copy(
-            obuf.at[k],
-            out_ref.at[:, :, pl.ds(pl.multiple_of(k * span_lanes, span_lanes), span_lanes)],
-            out_sem.at[k],
-        )
 
     def convolve(k):
         def one(n, _):
@@ -246,11 +238,10 @@
                 for r in range(2):
                     row = scen * r + s
                     total = total + fade[b, r] * carry[k, row : row + 1, lanes]
-                obuf[k, s, :, lanes] = total.astype(jnp.bfloat16)
+                out_ref[s, :, pl.ds(pl.multiple_of(b * width, width), width)] = total.astype(jnp.bfloat16)
             return 0
 
         lax.fori_loop(0, CHUNK, one, 0, unroll=UNROLL_C)
-        out_copy(k).start()
 
     lag = jnp.minimum(LAG + LAG_PAIR * pair, 2 * chunks)
     delay = jnp.maximum(lag, chunks)
@@ -280,7 +271,6 @@
     lax.fori_loop(0, chunks + delay, step, 0)
 
     def drain(k, _):
-        out_copy(k).wait()
         peer_copy(k).wait_send()
 
         @pl.when(has_next)
@@ -305,7 +295,7 @@
         functools.partial(kernel, pairs),
         out_shape=pltpu.VMEM((scen, steps, blocks * width), jnp.bfloat16),
         in_specs=[hbm] * 6,
-        out_specs=pl.BlockSpec(memory_space=pl.ANY),
+        out_specs=pl.BlockSpec(memory_space=pltpu.VMEM),
         scratch_shapes=[
             pltpu.SMEM((slots, blocks), jnp.int32),
             pltpu.VMEM((blocks, width), jnp.int32),
@@ -326,11 +316,9 @@
             pltpu.VMEM((16, time_const.shape[0]), jnp.float32),
             pltpu.VMEM((2 * steps, 4 * steps), jnp.bfloat16),
             pltpu.VMEM((blocks, scen, steps, width), jnp.float32),
-            pltpu.VMEM((chunks, scen, steps, lanes), jnp.bfloat16),
             dma((4,)),
             dma((lines // panel,)),
             dma,
-            dma((chunks,)),
             dma((lines // panel,)),
             dma((lines // panel,)),
             dma((chunks,)),

time: 24.7 us -> 24.3 us (0.984)
  Pallas kernels: 22.7 us -> 22.4 us
    pallas_call x1, Pallas kernels: 22.7 us -> 22.4 us  [body(): pl.pallas_call(functools.partial(kernel, pairs), out_shape=pltpu.VMEM((sc...]
where the time goes in v2:
time: 24.3 us; the launch traced here: 24 us
  Pallas kernels  22.4 us (92%)
  local copies, waits for them, and re-layouts  1.67 us (7%)
    pallas_call x1, Pallas kernels, body(): pl.pallas_call(functools.partial(kernel, pairs), out_shape=pltpu.VMEM((sc...  22.4 us
    unnamed x1, local copies, waits for them, and re-layouts  1.67 us

profile of v2, /device:TPU:26, one launch (start us, length us, event | category | flops | bytes accessed | tf_op | source)
XLA Modules:
  0.0 24.0 jit_solution(6267507885618767142)
XLA Ops:
  0.0 22.4 %shard_map.64 = bf16[4,64,6144]{2,1,0:T(8,128)(2,1)S(1)} custom-call(bf16[4,64,4096]{2,1,0:T(8,128)(2,1)} %volt_ref.1, bf16[48,512,128]{2,1,0:T(8,128)(2,1)} %bitcast.5, s32[4,48]{1,0:T(4,128)} %bitcast.7, s32[48,128]{1,0:T(8,128)} %bitcast.6, f32[2,256]{1,0:T(2,128)} %bitcast.8, f32[2,256]{1,0:T(2,128)} %bitcast.9), custom_call_target="tpu_custom_call" | custom-call | tf_op jit(solution)/shard_map/pallas_call | solution.py:294
  22.4 1.7 %copy.8 = bf16[4,64,6144]{2,1,0:T(8,128)(2,1)} copy(bf16[4,64,6144]{2,1,0:T(8,128)(2,1)S(1)} %shard_map.64) | data formatting | bytes 6291456
